TPU v7x, 32 devices: a whole 2x2x4 slice. The times are simulated.
32 devices in a mesh: groups: 2 (over y), sig: 4 (over z), build: 4 (over x, core).
Axes of the slice: x: 2, y: 2, z: 4, core: 2. Of those that a mesh axis runs over, the one named last changes fastest.
Arguments:
- tiles: bfloat16 [8, 4, 32, 256, 256], P(('groups', 'sig'), 'build'), parts along dimension 0, may hold values from 0 to 15, as said below
- tile_rows: int32 [8, 4, 32], P(('groups', 'sig'), 'build'), parts along dimension 0, may hold values from 0 to 7, as said below
- tile_cols: int32 [8, 4, 32], P(('groups', 'sig'), 'build'), parts along dimension 0, may hold values from 0 to 7
- tile_count: int32 [8, 4], P(('groups', 'sig'), 'build'), parts along dimension 0, may hold values from 1 to 32, as said below
- factor_w: bfloat16 [16384, 128], P(('groups', 'sig', 'build')), parts along dimension 0, as said below
- factor_h: bfloat16 [16384, 128], P(('groups', 'sig', 'build')), parts along dimension 0, as said below
- tv_weight: float32 [256], P('groups'), parts along dimension 0, may hold values from 0.05 to 0.6
Outputs:
- w_new: bfloat16 [16384, 128], P(('groups', 'sig', 'build')), parts along dimension 0
- smooth: float32 [16384, 128], P(('groups', 'sig', 'build')), parts along dimension 0
There are 2 independent parts, one for each index of `groups`. A program takes and returns all parts, laid end to end along the dimension named above; each array names one. Nothing has to cross between parts.
Inputs may be any that keep to these rules, and one draw needn't show every extreme that they name: `tiles`: nonnegative integer counts. Within one block all slots name distinct (tile_rows, tile_cols) pairs. Slots from tile_count on hold no data; some block uses all 32 slots. `factor_w`: positive entries. `factor_h`: positive entries.
All inputs are finite; a program needn't handle non-finite values.
Results may differ from a plain program's by a relative error of at most 0.0045.
Values may be sent and summed in bfloat16 or wider, within the bound.
A program may use at most 64 MiB of HBM per device.

v0:
```python
import jax
import jax.numpy as jnp
from jax import lax
from jax.sharding import PartitionSpec as P

TV_STEPS = 16


TAU = 0.25


def with_halo(block, sides, width):
    for axis, dim in sides:
        count = lax.axis_size(axis)
        forward = [(i, i + 1) for i in range(count - 1)]
        backward = [(target, source) for source, target in forward]
        low = lax.ppermute(
            lax.slice_in_dim(block, block.shape[dim] - width, None, axis=dim), axis, forward
        )
        high = lax.ppermute(lax.slice_in_dim(block, 0, width, axis=dim), axis, backward)
        block = jnp.concatenate([low, block, high], axis=dim)
    return block


def grand_total(values):
    return lax.psum(values, ("sig", "build"))


def column_block(shard):
    return lax.all_gather(shard, "sig", axis=0, tiled=True)


def dual_sweeps(ext_signal, ext_dual, keep_mask, sweeps, tv_weight):
    for repeat in range(sweeps):
        primal = ext_signal[1:] - ext_dual[:-1] + ext_dual[1:]
        ext_dual = (
            jnp.clip(ext_dual[1:-1] + TAU * (primal[1:] - primal[:-1]), -tv_weight, tv_weight)
            * keep_mask[1:-1]
        )
        ext_signal = ext_signal[1:-1]
        keep_mask = keep_mask[1:-1]
    smooth_next = ext_signal[1:-1] - ext_dual[:-2] + ext_dual[1:-1]
    return (ext_dual[1:-1], smooth_next)


def local(tiles, tile_rows, tile_cols, tile_count, factor_w, factor_h, tv_weight):
    block_tiles = tiles[0, 0]
    rows_index = tile_rows[0, 0]
    cols_index = tile_cols[0, 0]
    slot_count = block_tiles.shape[0]
    tile_size = block_tiles.shape[1]
    rank_width = factor_w.shape[1]
    live_mask = (jnp.arange(slot_count) < tile_count[0, 0])[:, None, None]
    col_total = grand_total(jnp.sum(factor_w.astype(jnp.float32), axis=0))
    row_block = lax.all_gather(factor_w, "build", axis=0, tiled=True)
    row_tiles = row_block.shape[0] // tile_size
    w_chosen = jnp.take(row_block.reshape(row_tiles, tile_size, rank_width), rows_index, axis=0)

    def ratios(h_block):
        col_count = h_block.shape[0] // tile_size
        h_chosen = jnp.take(h_block.reshape(col_count, tile_size, rank_width), cols_index, axis=0)
        product = jnp.einsum("sik,sjk->sij", w_chosen, h_chosen, preferred_element_type=jnp.float32)
        ratio_tile = jnp.where(live_mask, block_tiles.astype(jnp.float32) / product, 0.0).astype(
            jnp.bfloat16
        )
        return (h_chosen, ratio_tile)

    h_block = column_block(factor_h)
    col_tiles = h_block.shape[0] // tile_size
    h_chosen, ratio_tile = ratios(h_block)
    contrib = jnp.einsum("sij,sik->sjk", ratio_tile, w_chosen, preferred_element_type=jnp.float32)
    col_onehot = (cols_index[:, None] == jnp.arange(col_tiles)[None, :]).astype(jnp.float32)
    numer_h = jnp.einsum(
        "sc,sjk->cjk", col_onehot, contrib, precision=lax.Precision.HIGHEST
    ).reshape(-1, rank_width)
    share_h = lax.psum_scatter(numer_h, "sig", scatter_dimension=0, tiled=True)
    h_new = (factor_h.astype(jnp.float32) * share_h / col_total).astype(jnp.bfloat16)
    h_block_new = column_block(h_new)
    h_chosen_new, ratio_new = ratios(h_block_new)
    contrib_w = jnp.einsum(
        "sij,sjk->sik", ratio_new, h_chosen_new, preferred_element_type=jnp.float32
    )
    row_onehot = (rows_index[:, None] == jnp.arange(row_tiles)[None, :]).astype(jnp.float32)
    numer_w = jnp.einsum(
        "sr,sik->rik", row_onehot, contrib_w, precision=lax.Precision.HIGHEST
    ).reshape(-1, rank_width)
    share_w = lax.psum_scatter(numer_w, "build", scatter_dimension=0, tiled=True)
    row_total = grand_total(jnp.sum(h_new.astype(jnp.float32), axis=0))
    w_new = (factor_w.astype(jnp.float32) * share_w / row_total).astype(jnp.bfloat16)
    signal = h_new.astype(jnp.float32)
    shard_width = signal.shape[0]
    anchor = lax.axis_index(("sig", "build")) * shard_width
    total_cols = shard_width * lax.axis_size(("sig", "build"))
    ext_signal = with_halo(signal, ((("sig", "build"), 0),), TV_STEPS + 1)
    position = anchor - (TV_STEPS + 1) + jnp.arange(shard_width + 2 * TV_STEPS + 2)
    dual_final, smooth = dual_sweeps(
        ext_signal,
        jnp.zeros_like(ext_signal),
        ((position >= 0) & (position < total_cols - 1)).astype(jnp.float32)[:, None],
        TV_STEPS,
        tv_weight,
    )
    return (w_new, smooth)


def solution(mesh):
    return jax.shard_map(
        local,
        mesh=mesh,
        in_specs=(
            P(("groups", "sig"), "build", None, None, None),
            P(("groups", "sig"), "build", None),
            P(("groups", "sig"), "build", None),
            P(("groups", "sig"), "build"),
            P(("groups", "sig", "build"), None),
            P(("groups", "sig", "build"), None),
            P("groups"),
        ),
        out_specs=(P(("groups", "sig", "build"), None), P(("groups", "sig", "build"), None)),
        check_vma=False,
    )
```

profile of v0, /device:TPU:1, one launch (start us, length us, event | category | flops | bytes accessed | tf_op | source)
XLA Modules:
  0.0 166.7 jit_solution(2847859683761877728)
XLA Ops:
  7.2 0.7 compare_select_fusion.1
  7.9 0.7 compare_select_fusion
  8.5 0.7 compare_and_fusion
  9.9 15.5 %all_gather.10 = bf16[2048,128]{1,0:T(8,128)(2,1)S(1)} all-gather(bf16[512,128]{1,0:T(8,128)(2,1)} %param.14), channel_id=1, replica_groups=mesh['groups'=2,'sig'=4,'build'=4] {'sig'}, dimensions={0}, use_global_device_ids=true | all-gather | bytes 655360 | tf_op jit(solution)/shard_map/all_gather | solution.py:30
  25.4 9.3 %all_gather.9 = bf16[2048,128]{1,0:T(8,128)(2,1)S(1)} all-gather(bf16[512,128]{1,0:T(8,128)(2,1)} %param.13), channel_id=1, replica_groups=mesh['groups'=2,'sig'=4,'build'=4] {'build'}, dimensions={0}, use_global_device_ids=true | all-gather | bytes 655360 | tf_op jit(solution)/shard_map/all_gather | solution.py:55
  34.7 0.9 gather_fusion
  35.7 2.1 %gather_fusion.1 = bf16[32,256,128]{2,1,0:T(8,128)(2,1)} fusion(bf16[8,256,128]{2,1,0:T(8,128)(2,1)S(1)} %bitcast.28, s32[1024]{0:T(1024)S(1)} %pad_clamp_fusion), kind=kCustom, calls=%fused_computation.1.clone | custom fusion | bytes 4194432 | tf_op jit(solution)/shard_map/jit(_take)/gather | solution.py:61
  37.8 7.7 %fusion.10 = f32[32,256,128]{2,1,0:T(8,128)} fusion(bf16[1,1,32,256,256]{4,3,2,1,0:T(8,128)(2,1)} %param.9, pred[32]{0:T(512)(128)(4,1)S(1)} %iota_compare_fusion.2, bf16[32,256,128]{2,1,0:T(8,128)(2,1)} %gather_fusion.1, pred[32]{0:T(512)(128)(4,1)S(1)} %get-tuple-element.9, bf16[32,256,128]{2,1,0:T(8,128)(2,1)S(1)} %gather_fusion, ...), kind=kOutput, calls=%fused_computation.14 | convolution fusion | flops 1085276160 | bytes 12583008 | tf_op jit(solution)/shard_map/sij,sik->sjk/dot_general | solution.py:71
  45.5 5.8 %fusion.6 = f32[8,256,128]{2,0,1:T(8,128)S(1)} fusion(f32[32,256,128]{2,1,0:T(8,128)} %fusion.10, s32[32]{0:T(128)S(1)} %bitcast.32), kind=kOutput, calls=%fused_computation.11 | convolution fusion | flops 100663552 | bytes 5243008 | tf_op jit(solution)/shard_map/sc,sjk->cjk/dot_general | solution.py:73
  51.4 1.2 copy.9
  53.9 29.8 %psum.14 = f32[128]{0:T(128)S(1)} all-reduce(f32[128]{0:T(128)S(1)} %convert_reduce_fusion), channel_id=1, replica_groups=mesh['groups'=2,'sig'=4,'build'=4] {'sig','build'}, use_global_device_ids=true, to_apply=%region_2.0 | all-reduce | flops 128 | bytes 1024 | tf_op jit(solution)/shard_map/psum | solution.py:26
  83.7 1.0 fusion.127
  84.7 13.3 %all_gather.11 = bf16[2048,128]{1,0:T(8,128)(2,1)S(1)} all-gather(bf16[512,128]{1,0:T(8,128)(2,1)S(1)} %get-tuple-element.4), channel_id=1, replica_groups=mesh['groups'=2,'sig'=4,'build'=4] {'sig'}, dimensions={0}, use_global_device_ids=true | all-gather | bytes 655360 | tf_op jit(solution)/shard_map/all_gather | solution.py:30
  98.0 5.2 %collective-permute-start = (f32[17,128]{1,0:T(8,128)S(1)}, f32[17,128]{1,0:T(8,128)S(1)}, u32[]{:S(2)}, u32[]{:S(2)}) collective-permute-start(f32[17,128]{1,0:T(8,128)S(1)} %get-tuple-element.7), channel_id=1, source_target_pairs={{0,1},{1,2},{2,3},{3,4},{4,5},{5,6},{6,7},{7,8},{8,9},{9,10},{10,1... | collective-permute-start | bytes 26120 | tf_op jit(solution)/shard_map/ppermute | solution.py:17
  103.2 5.5 %collective-permute-start.1 = (f32[17,128]{1,0:T(8,128)S(1)}, f32[17,128]{1,0:T(8,128)S(1)}, u32[]{:S(2)}, u32[]{:S(2)}) collective-permute-start(f32[17,128]{1,0:T(8,128)S(1)} %get-tuple-element.8), channel_id=1, source_target_pairs={{1,0},{2,1},{3,2},{4,3},{5,4},{6,5},{7,6},{8,7},{9,8},{10,9},{11,1... | collective-permute-start | bytes 26120 | tf_op jit(solution)/shard_map/ppermute | solution.py:20
  108.6 2.1 %gather_fusion.2 = bf16[32,256,128]{2,1,0:T(8,128)(2,1)} fusion(bf16[8,256,128]{2,1,0:T(8,128)(2,1)S(1)} %bitcast.27, s32[1024]{0:T(1024)S(1)} %pad_clamp_fusion), kind=kCustom, calls=%fused_computation.2.clone | custom fusion | bytes 4194432 | tf_op jit(solution)/shard_map/jit(_take)/gather | solution.py:61
  110.8 7.9 %fusion.8 = f32[32,256,128]{2,1,0:T(8,128)} fusion(bf16[1,1,32,256,256]{4,3,2,1,0:T(8,128)(2,1)} %param.9, pred[32]{0:T(512)(128)(4,1)S(1)} %iota_compare_fusion.2, bf16[32,256,128]{2,1,0:T(8,128)(2,1)} %gather_fusion.2, pred[32]{0:T(512)(128)(4,1)S(1)} %get-tuple-element.9, bf16[32,256,128]{2,1,0:T(8,128)(2,1)S(1)} %gather_fusion, ...), kind=kOutput, calls=%fused_computation.13 | convolution fusion | flops 1085276160 | bytes 12583008 | tf_op jit(solution)/shard_map/sij,sjk->sik/dot_general | solution.py:80
  118.7 5.8 %fusion.4 = f32[8,256,128]{2,0,1:T(8,128)S(1)} fusion(f32[32,256,128]{2,1,0:T(8,128)} %fusion.8, s32[32]{0:T(128)S(1)} %bitcast.33), kind=kOutput, calls=%fused_computation.9 | convolution fusion | flops 100663552 | bytes 5243008 | tf_op jit(solution)/shard_map/sr,sik->rik/dot_general | solution.py:84
  124.5 1.2 copy.10
  126.0 0.1 fusion.44
  126.2 0.1 fusion.39
  126.4 0.1 fusion.34
  126.8 0.1 fusion.63
  127.0 0.1 fusion.58
  127.2 0.1 fusion.53
  127.4 0.1 fusion.88
  127.9 0.1 fusion.78
  128.7 0.1 fusion.98
  128.9 0.1 fusion.93
  129.1 0.8 slice_add_fusion.15
  129.8 28.4 %psum.15 = f32[128]{0:T(128)S(1)} all-reduce(f32[128]{0:T(128)S(1)} %get-tuple-element.6), channel_id=1, replica_groups=mesh['groups'=2,'sig'=4,'build'=4] {'sig','build'}, use_global_device_ids=true, to_apply=%region_5.7 | all-reduce | flops 128 | bytes 1024 | tf_op jit(solution)/shard_map/psum | solution.py:26
  158.2 1.6 fusion.110
  (63 shorter events, 3.2 us)
Async XLA Ops:
  7.2 76.5 %reduce-scatter.3.cloned.1.call-start = ((), (), s32[]{:S(2)}) async-start(), calls=%async_computation.2 | async-start | bytes 1310720 | tf_op jit(solution)/shard_map/reduce_scatter | solution.py:76
  37.8 7.7 %copy-start.3 = (s32[1,1,32]{2,1,0:T(1,128)S(1)}, s32[1,1,32]{2,1,0:T(1,128)}, u32[]{:S(2)}) copy-start(s32[1,1,32]{2,1,0:T(1,128)} %param.11) | copy-start | bytes 388
  51.3 2.5 %copy-start.2 = (f32[128]{0:T(128)S(1)}, f32[128]{0:T(128)}, u32[]{:S(2)}) copy-start(f32[128]{0:T(128)} %param.15) | copy-start | bytes 1540
  51.3 2.5 %copy-start = (bf16[512,128]{1,0:T(8,128)(2,1)S(1)}, bf16[512,128]{1,0:T(8,128)(2,1)}, u32[]{:S(2)}) copy-start(bf16[512,128]{1,0:T(8,128)(2,1)} %param.13) | copy-start | bytes 393220
  51.3 32.3 %copy-start.1 = (bf16[512,128]{1,0:T(8,128)(2,1)S(1)}, bf16[512,128]{1,0:T(8,128)(2,1)}, u32[]{:S(2)}) copy-start(bf16[512,128]{1,0:T(8,128)(2,1)} %param.14) | copy-start | bytes 393220
  52.6 105.7 %reduce-scatter.5.cloned.1.call-start = ((), (), s32[]{:S(2)}) async-start(), calls=%async_computation.3 | async-start | bytes 1310720 | tf_op jit(solution)/shard_map/reduce_scatter | solution.py:87
  98.0 27.7 %collective-permute-start = (f32[17,128]{1,0:T(8,128)S(1)}, f32[17,128]{1,0:T(8,128)S(1)}, u32[]{:S(2)}, u32[]{:S(2)}) collective-permute-start(f32[17,128]{1,0:T(8,128)S(1)} %get-tuple-element.7), channel_id=1, source_target_pairs={{0,1},{1,2},{2,3},{3,4},{4,5},{5,6},{6,7},{7,8},{8,9},{9,10},{10,1... | collective-permute-start | bytes 26120 | tf_op jit(solution)/shard_map/ppermute | solution.py:17
  103.2 22.6 %collective-permute-start.1 = (f32[17,128]{1,0:T(8,128)S(1)}, f32[17,128]{1,0:T(8,128)S(1)}, u32[]{:S(2)}, u32[]{:S(2)}) collective-permute-start(f32[17,128]{1,0:T(8,128)S(1)} %get-tuple-element.8), channel_id=1, source_target_pairs={{1,0},{2,1},{3,2},{4,3},{5,4},{6,5},{7,6},{8,7},{9,8},{10,9},{11,1... | collective-permute-start | bytes 26120 | tf_op jit(solution)/shard_map/ppermute | solution.py:20
  110.8 7.9 %copy-start.4 = (s32[1,1,32]{2,1,0:T(1,128)S(1)}, s32[1,1,32]{2,1,0:T(1,128)}, u32[]{:S(2)}) copy-start(s32[1,1,32]{2,1,0:T(1,128)} %param.10) | copy-start | bytes 388
Sparse Core Ops, SparseCore 0:
  52.7 27.8 reduce-scatter.2
  125.8 25.2 reduce-scatter.4
where the time goes:
time: 169 us; the launch traced here: 167 us
  blocking collectives  96.3 us (57%)
  matrix products  27.2 us (16%)
  between operations  15 us (9%)
  starting transfers between devices  10.7 us (6%)
  local copies, waits for them, and re-layouts  8.78 us (5%)
  other arithmetic  8.69 us (5%)
    psum x2, blocking collectives, grand_total(): return lax.psum(values, ('sig', 'build'))  58.2 us
    all_gather x2, blocking collectives, column_block(): return lax.all_gather(shard, 'sig', axis=0, tiled=True)  28.8 us
    all_gather x1, blocking collectives, local(): row_block = lax.all_gather(factor_w, 'build', axis=0, tiled=True)  9.32 us
    dot_general x1, matrix products, local(): jnp.einsum('sij,sjk->sik', ratio_new, h_chosen_new, preferred_element_typ...  7.9 us
    dot_general x1, matrix products, local(): jnp.einsum('sij,sik->sjk', ratio_tile, w_chosen, preferred_element_type=j...  7.67 us
    dot_general x1, matrix products, local(): jnp.einsum('sc,sjk->cjk', col_onehot, contrib, precision=lax.Precision.HI...  5.81 us
    dot_general x1, matrix products, local(): jnp.einsum('sr,sik->rik', row_onehot, contrib_w, precision=lax.Precision....  5.81 us
    ppermute x1, starting transfers between devices, with_halo(): lax.ppermute(lax.slice_in_dim(block, 0, width, axis=dim), axis, backward)  5.47 us
  transfers between devices with their start and end apart: 4, of which 0 were waited for; matrix products, arithmetic and copies ran while one was open for 13% of the time, Pallas kernels for 0%

commit v1 on v0

v1 whole, which is shorter than its diff:
```python
import functools

import jax
import jax.numpy as jnp
from jax import lax
from jax.experimental import pallas as pl
from jax.experimental.pallas import tpu as pltpu
from jax.sharding import PartitionSpec as P

TV_STEPS = 16
TAU = 0.25
HALO = 32
GROUP = 4
MESH = pl.DeviceIdType.MESH


def kernel(
    n_sig, n_build,
    meta, tiles_hbm, fw_ref, fh_ref, tv_ref,
    w_out, smooth_out,
    tiles, w_blk, w_turn, h_blk, h_next, w_tiles, h_tiles, chain_h, chain_w, numer,
    h_send, h_recv, w_send, w_recv, col_part, row_part, ext,
    tile_sem, send_w, recv_w, send_h, recv_h, send_ct, recv_ct, send_nh, recv_nh,
    send_h2, recv_h2, send_halo, recv_halo, send_rt, recv_rt, send_nw, recv_nw,
):
    f32, bf16 = jnp.float32, jnp.bfloat16
    sig = lax.axis_index("sig")
    build = lax.axis_index("build")
    slots, tile = tiles.shape[0], tiles.shape[1]
    w_rows, h_rows = fw_ref.shape[0], fh_ref.shape[0]
    row_tiles = w_blk.shape[0] // tile
    col_tiles = h_blk.shape[0] // tile

    load = pltpu.make_async_copy(tiles_hbm, tiles, tile_sem)
    load.start()

    def sig_peer(k):
        return lax.rem(sig + k, n_sig)

    def build_peer(k):
        return lax.rem(build + k, n_build)

    total = n_sig * n_build
    index = sig * n_build + build
    above = lax.rem(index + 1, total)
    below = lax.rem(index + total - 1, total)

    def at(linear):
        return {"sig": lax.div(linear, n_build), "build": lax.rem(linear, n_build)}

    barrier = pltpu.get_barrier_semaphore()
    for k in range(1, n_sig):
        pl.semaphore_signal(barrier, inc=1, device_id={"sig": sig_peer(k)}, device_id_type=MESH)
    for k in range(1, n_build):
        pl.semaphore_signal(barrier, inc=1, device_id={"build": build_peer(k)}, device_id_type=MESH)
    pl.semaphore_signal(barrier, inc=1, device_id=at(above), device_id_type=MESH)
    pl.semaphore_signal(barrier, inc=1, device_id=at(below), device_id_type=MESH)
    pl.semaphore_wait(barrier, n_sig + n_build)

    def remote(src, dst, send, recv, device):
        copy = pltpu.make_async_remote_copy(
            src_ref=src, dst_ref=dst, send_sem=send, recv_sem=recv,
            device_id=device, device_id_type=MESH,
        )
        copy.start()
        return copy

    def rows_of(place, rows):
        return pl.ds(pl.multiple_of(place * rows, rows), rows)

    pending = []

    h_copies = [
        remote(fh_ref, h_blk.at[rows_of(sig, h_rows)], send_h.at[k], recv_h.at[k], {"sig": sig_peer(k)})
        for k in range(1, n_sig)
    ]
    w_copies = [
        remote(fw_ref, w_blk.at[rows_of(build, w_rows)], send_w.at[k], recv_w.at[k], {"build": build_peer(k)})
        for k in range(1, n_build)
    ]
    pending += h_copies + w_copies
    h_blk[rows_of(sig, h_rows), :] = fh_ref[...]
    w_blk[rows_of(build, w_rows), :] = fw_ref[...]
    chain_h[0] = jnp.zeros(chain_h.shape[1:], f32)
    chain_w[0] = jnp.zeros(chain_w.shape[1:], f32)

    for copy in w_copies:
        copy.wait_recv()
    part = jnp.zeros((8, w_blk.shape[1]), f32)
    for r in range(row_tiles):
        block = w_blk[r * tile:(r + 1) * tile, :]
        w_tiles[r] = block
        w_turn[r] = block.T
        part += block.astype(f32).reshape(tile // 8, 8, -1).sum(axis=0)
    col_part[sig] = part
    ct_copies = [
        remote(col_part.at[sig], col_part.at[sig], send_ct.at[k], recv_ct.at[k], {"sig": sig_peer(k)})
        for k in range(1, n_sig)
    ]
    pending += ct_copies

    load.wait()
    for copy in h_copies:
        copy.wait_recv()
    for c in range(col_tiles):
        h_tiles[0, c] = h_blk[c * tile:(c + 1) * tile, :]

    def ratio_of(slot, w, h):
        product = lax.dot_general(w, h, (((1,), (1,)), ((), ())), preferred_element_type=f32)
        return (tiles[slot].astype(f32) / product).astype(bf16)

    def pass_h(step, carry):
        terms = []
        for g in range(GROUP):
            slot = step * GROUP + g
            row, col = meta[0, slot], meta[1, slot]
            ratio = ratio_of(slot, w_tiles[row], h_tiles[0, col])
            terms.append(jnp.dot(w_turn[row], ratio, preferred_element_type=f32))
        for g in range(GROUP):
            slot = step * GROUP + g
            chain_h[slot + 1] = chain_h[meta[1, slots + slot]] + terms[g]
        return carry

    lax.fori_loop(0, slots // GROUP, pass_h, 0)
    for c in range(col_tiles):
        block = chain_h[meta[1, 2 * slots + c]].T
        numer[c * tile:(c + 1) * tile, :] = block
        h_send[c * tile:(c + 1) * tile, :] = block.astype(bf16)
    nh_copies = [
        remote(h_send.at[rows_of(sig_peer(k), h_rows)], h_recv.at[sig], send_nh.at[k], recv_nh.at[k],
               {"sig": sig_peer(k)})
        for k in range(1, n_sig)
    ]
    pending += nh_copies
    for copy in ct_copies:
        copy.wait_recv()
    col_sum = col_part[0]
    for k in range(1, n_sig):
        col_sum += col_part[k]
    col_total = jnp.sum(col_sum, axis=0, keepdims=True)
    share = numer[rows_of(sig, h_rows), :]
    for k in range(1, n_sig):
        nh_copies[k - 1].wait_recv()
        share += h_recv[sig_peer(n_sig - k)].astype(f32)
    h_new = (fh_ref[...].astype(f32) * share / col_total).astype(bf16)
    mine = rows_of(sig, h_rows)
    h_next[mine, :] = h_new
    ext[HALO:HALO + h_rows, :] = h_new
    halo_copies = [
        remote(ext.at[h_rows:HALO + h_rows], ext.at[0:HALO], send_halo.at[0], recv_halo.at[0], at(above)),
        remote(ext.at[HALO:2 * HALO], ext.at[HALO + h_rows:2 * HALO + h_rows],
               send_halo.at[1], recv_halo.at[1], at(below)),
    ]
    h2_copies = [
        remote(h_next.at[mine], h_next.at[mine], send_h2.at[k], recv_h2.at[k], {"sig": sig_peer(k)})
        for k in range(1, n_sig)
    ]
    pending += halo_copies + h2_copies

    for copy in halo_copies:
        copy.wait_recv()
    signal = ext[...].astype(f32)
    length = signal.shape[0]
    position = index * h_rows - HALO + lax.broadcasted_iota(jnp.int32, signal.shape, 0)
    keep = (position >= 0) & (position < total * h_rows - 1)
    limit = jnp.where(keep, jnp.broadcast_to(tv_ref[...], signal.shape), 0.0)
    pull = TAU * (pltpu.roll(signal, length - 1, 0) - signal)

    def sweep(step, dual):
        around = pltpu.roll(dual, 1, 0) + pltpu.roll(dual, length - 1, 0)
        moved = pull + (1.0 - 2.0 * TAU) * dual + TAU * around
        return jnp.maximum(jnp.minimum(moved, limit), -limit)

    dual = lax.fori_loop(0, TV_STEPS, sweep, jnp.zeros_like(signal))
    smooth = signal - pltpu.roll(dual, 1, 0) + dual
    smooth_out[...] = smooth[HALO:HALO + h_rows, :]

    for copy in h2_copies:
        copy.wait_recv()
    part = jnp.zeros((8, w_blk.shape[1]), f32)
    for c in range(col_tiles):
        block = h_next[c * tile:(c + 1) * tile, :]
        h_tiles[1, c] = block
        part += block.astype(f32).reshape(tile // 8, 8, -1).sum(axis=0)
    row_part[build] = part
    rt_copies = [
        remote(row_part.at[build], row_part.at[build], send_rt.at[k], recv_rt.at[k], {"build": build_peer(k)})
        for k in range(1, n_build)
    ]
    pending += rt_copies

    def pass_w(step, carry):
        terms = []
        for g in range(GROUP):
            slot = step * GROUP + g
            h = h_tiles[1, meta[1, slot]]
            ratio = ratio_of(slot, w_tiles[meta[0, slot]], h)
            terms.append(jnp.dot(ratio, h, preferred_element_type=f32))
        for g in range(GROUP):
            slot = step * GROUP + g
            chain_w[slot + 1] = chain_w[meta[0, slots + slot]] + terms[g]
        return carry

    lax.fori_loop(0, slots // GROUP, pass_w, 0)
    for r in range(row_tiles):
        block = chain_w[meta[0, 2 * slots + r]]
        numer[r * tile:(r + 1) * tile, :] = block
        w_send[r * tile:(r + 1) * tile, :] = block.astype(bf16)
    nw_copies = [
        remote(w_send.at[rows_of(build_peer(k), w_rows)], w_recv.at[build], send_nw.at[k], recv_nw.at[k],
               {"build": build_peer(k)})
        for k in range(1, n_build)
    ]
    pending += nw_copies
    for copy in rt_copies:
        copy.wait_recv()
    row_sum = row_part[0]
    for k in range(1, n_build):
        row_sum += row_part[k]
    row_total = jnp.sum(row_sum, axis=0, keepdims=True)
    share = numer[rows_of(build, w_rows), :]
    for k in range(1, n_build):
        nw_copies[k - 1].wait_recv()
        share += w_recv[build_peer(n_build - k)].astype(f32)
    w_out[...] = (fw_ref[...].astype(f32) * share / row_total).astype(bf16)
    for copy in pending:
        copy.wait_send()


def links(index, tiles, count):
    slot = jnp.arange(index.shape[0], dtype=jnp.int32)
    same = (index[:, None] == index[None, :]) & (slot[None, :] < slot[:, None]) & (slot[None, :] < count)
    before = jnp.max(jnp.where(same, slot[None, :] + 1, 0), axis=1)
    hit = (jnp.arange(tiles, dtype=jnp.int32)[:, None] == index[None, :]) & (slot[None, :] < count)
    last = jnp.max(jnp.where(hit, slot[None, :] + 1, 0), axis=1)
    return jnp.concatenate([index, before, last])


def local(n_sig, n_build, tiles, tile_rows, tile_cols, tile_count, factor_w, factor_h, tv_weight):
    tiles = tiles[0, 0]
    slots, tile = tiles.shape[:2]
    w_rows, rank = factor_w.shape
    h_rows = factor_h.shape[0]
    block_rows, block_cols = w_rows * n_build, h_rows * n_sig
    most = max(block_rows, block_cols) // tile
    live = tile_count[0, 0]
    meta = jnp.stack([links(tile_rows[0, 0], most, live), links(tile_cols[0, 0], most, live)])
    vmem, smem = pltpu.VMEM, pltpu.SMEM
    f32, bf16 = jnp.float32, jnp.bfloat16
    dma = pltpu.SemaphoreType.DMA
    in_vmem = pl.BlockSpec(memory_space=pltpu.VMEM)
    in_smem = pl.BlockSpec(memory_space=pltpu.SMEM)
    return pl.pallas_call(
        functools.partial(kernel, n_sig, n_build),
        out_shape=(
            jax.ShapeDtypeStruct((w_rows, rank), bf16),
            jax.ShapeDtypeStruct((h_rows, rank), f32),
        ),
        in_specs=[in_smem, pl.BlockSpec(memory_space=pl.ANY), in_vmem, in_vmem, in_vmem],
        out_specs=(in_vmem, in_vmem),
        scratch_shapes=[
            vmem((slots, tile, tile), bf16),
            vmem((block_rows, rank), bf16),
            vmem((block_rows // tile, rank, tile), bf16),
            vmem((block_cols, rank), bf16),
            vmem((block_cols, rank), bf16),
            vmem((block_rows // tile, tile, rank), bf16),
            vmem((2, block_cols // tile, tile, rank), bf16),
            vmem((slots + 1, rank, tile), f32),
            vmem((slots + 1, tile, rank), f32),
            vmem((max(block_rows, block_cols), rank), f32),
            vmem((block_cols, rank), bf16),
            vmem((n_sig, h_rows, rank), bf16),
            vmem((block_rows, rank), bf16),
            vmem((n_build, w_rows, rank), bf16),
            vmem((n_sig, 8, rank), f32),
            vmem((n_build, 8, rank), f32),
            vmem((h_rows + 2 * HALO, rank), bf16),
            dma,
            dma((n_build,)), dma((n_build,)),
            dma((n_sig,)), dma((n_sig,)),
            dma((n_sig,)), dma((n_sig,)),
            dma((n_sig,)), dma((n_sig,)),
            dma((n_sig,)), dma((n_sig,)),
            dma((2,)), dma((2,)),
            dma((n_build,)), dma((n_build,)),
            dma((n_build,)), dma((n_build,)),
        ],
        compiler_params=pltpu.CompilerParams(
            collective_id=0, has_side_effects=True, vmem_limit_bytes=40 * 1024 * 1024
        ),
    )(meta, tiles, factor_w, factor_h, tv_weight[None, :])


def solution(mesh):
    return jax.shard_map(
        functools.partial(local, mesh.shape["sig"], mesh.shape["build"]),
        mesh=mesh,
        in_specs=(
            P(("groups", "sig"), "build", None, None, None),
            P(("groups", "sig"), "build", None),
            P(("groups", "sig"), "build", None),
            P(("groups", "sig"), "build"),
            P(("groups", "sig", "build"), None),
            P(("groups", "sig", "build"), None),
            P("groups"),
        ),
        out_specs=(P(("groups", "sig", "build"), None), P(("groups", "sig", "build"), None)),
        check_vma=False,
    )
```

time: 169 us -> 73.5 us (0.43)
  the two profiles are of different devices: /device:TPU:1 before, /device:TPU:21 now
where the time goes in v1:
time: 73.5 us; the launch traced here: 73.3 us
  Pallas kernels  63.5 us (86%)
  local copies, waits for them, and re-layouts  6 us (8%)
  other arithmetic  2.52 us (3%)
  between operations  1.32 us (2%)
    pallas_call x1, Pallas kernels, local(): pl.pallas_call(functools.partial(kernel, n_sig, n_build), out_shape=(jax....  63.5 us
    unnamed x10, local copies, waits for them, and re-layouts  6 us

profile of v1, /device:TPU:21, one launch (start us, length us, event | category | flops | bytes accessed | tf_op | source)
XLA Modules:
  0.0 73.3 jit_solution(3162586661946092708)
XLA Ops:
  1.3 0.8 %select_reduce_fusion.3 = (s32[8]{0:T(128)S(1)}, s32[8]{0:T(128)S(1)}) fusion(s32[32]{0:T(128)S(1)} %iota_add_fusion, s32[32]{0:T(128)} %bitcast.12, pred[32]{0:T(512)(128)(4,1)S(1)} %iota_compare_fusion.3, s32[32]{0:T(128)} %bitcast.15), kind=kLoop, calls=%fused_computation.9 | loop fusion | flops 2032 | bytes 480 | tf_op jit(solution)/shard_map/reduce_max | solution.py:235
  2.1 0.9 %select_reduce_fusion.1 = (s32[32]{0:T(128)S(1)}, s32[32]{0:T(128)S(1)}) fusion(s32[32]{0:T(128)S(1)} %iota_add_fusion, s32[32]{0:T(128)} %bitcast.13, pred[32]{0:T(512)(128)(4,1)S(1)} %iota_compare_fusion.3, s32[32]{0:T(128)} %bitcast.16), kind=kLoop, calls=%fused_computation.1 | loop fusion | flops 11200 | bytes 672 | tf_op jit(solution)/shard_map/reduce_max | solution.py:233
  3.1 0.8 %add_bitcast_fusion = (s32[1,72]{1,0:T(1,128)S(1)}, s32[1,72]{1,0:T(1,128)S(1)}) fusion(s32[8]{0:T(128)S(1)} %get-tuple-element.4, s32[32]{0:T(128)S(1)} %get-tuple-element.2, s32[32]{0:T(128)} %bitcast.14, s32[8]{0:T(128)S(1)} %get-tuple-element.5, s32[32]{0:T(128)S(1)} %get-tuple-element.3, s32[32]{0:T(128)} %bitcast.17), kind=kLoop, calls=%fused_computation.14 | loop fusion | flops 288 | bytes 1152 | tf_op jit(solution)/shard_map/stack | solution.py:247
  3.8 0.0 copy-start
  3.8 2.2 %copy-done = bf16[1,1,32,256,256]{4,3,2,1,0:T(8,128)(2,1)S(1)} copy-done((bf16[1,1,32,256,256]{4,3,2,1,0:T(8,128)(2,1)S(1)}, bf16[1,1,32,256,256]{4,3,2,1,0:T(8,128)(2,1)}, u32[]{:S(2)}) %copy-start) | copy-done | bytes 4194328
  6.0 0.0 copy-start.1
  6.0 0.9 %copy-done.1 = bf16[512,128]{1,0:T(8,128)(2,1)S(1)} copy-done((bf16[512,128]{1,0:T(8,128)(2,1)S(1)}, bf16[512,128]{1,0:T(8,128)(2,1)}, u32[]{:S(2)}) %copy-start.1) | copy-done | bytes 131096
  6.9 0.0 copy-start.2
  6.9 0.9 %copy-done.2 = bf16[512,128]{1,0:T(8,128)(2,1)S(1)} copy-done((bf16[512,128]{1,0:T(8,128)(2,1)S(1)}, bf16[512,128]{1,0:T(8,128)(2,1)}, u32[]{:S(2)}) %copy-start.2) | copy-done | bytes 131096
  7.8 0.0 copy-start.3
  7.8 0.7 copy-done.3
  8.5 63.5 %shard_map.86 = (bf16[512,128]{1,0:T(8,128)(2,1)S(1)}, f32[512,128]{1,0:T(8,128)S(1)}) custom-call(s32[2,72]{1,0:T(2,128)S(1)} %pad_add_fusion.meta, bf16[32,256,256]{2,1,0:T(8,128)(2,1)S(1)} %bitcast.10, bf16[512,128]{1,0:T(8,128)(2,1)S(1)} %copy-done.1, bf16[512,128]{1,0:T(8,128)(2,1)S(1)} %copy-done.2, f32[1,128]{1,0:T(1,128)S(1)} %bitcast.11), custom_call_target="tpu_custom_call" | custom-call | tf_op jit(solution)/shard_map/pallas_call | solution.py:253
  71.9 0.7 copy.12
  72.6 0.7 copy.13
  (3 shorter events, 0.0 us)
Async XLA Ops:
  3.8 2.2 %copy-start = (bf16[1,1,32,256,256]{4,3,2,1,0:T(8,128)(2,1)S(1)}, bf16[1,1,32,256,256]{4,3,2,1,0:T(8,128)(2,1)}, u32[]{:S(2)}) copy-start(bf16[1,1,32,256,256]{4,3,2,1,0:T(8,128)(2,1)} %param.7) | copy-start | bytes 12582916
  6.0 0.9 %copy-start.1 = (bf16[512,128]{1,0:T(8,128)(2,1)S(1)}, bf16[512,128]{1,0:T(8,128)(2,1)}, u32[]{:S(2)}) copy-start(bf16[512,128]{1,0:T(8,128)(2,1)} %fw_ref.1) | copy-start | bytes 393220
  6.9 0.9 %copy-start.2 = (bf16[512,128]{1,0:T(8,128)(2,1)S(1)}, bf16[512,128]{1,0:T(8,128)(2,1)}, u32[]{:S(2)}) copy-start(bf16[512,128]{1,0:T(8,128)(2,1)} %fh_ref.1) | copy-start | bytes 393220
  7.8 0.7 copy-start.3

commit v2 on v1

--- a/solution.py
+++ b/solution.py
@@ -10,17 +10,17 @@
 TV_STEPS = 16
 TAU = 0.25
 HALO = 32
-GROUP = 4
+GROUP = 8
 MESH = pl.DeviceIdType.MESH
 
 
 def kernel(
     n_sig, n_build,
-    meta, tiles_hbm, fw_ref, fh_ref, tv_ref,
+    rows_hbm, cols_hbm, count, tiles_hbm, fw_hbm, fh_hbm, tv_ref,
     w_out, smooth_out,
     tiles, w_blk, w_turn, h_blk, h_next, w_tiles, h_tiles, chain_h, chain_w, numer,
     h_send, h_recv, w_send, w_recv, col_part, row_part, ext,
-    tile_sem, send_w, recv_w, send_h, recv_h, send_ct, recv_ct, send_nh, recv_nh,
+    fw_ref, fh_ref, index_ref, link_ref, meta, tile_sem, local_sem, send_w, recv_w, send_h, recv_h, send_ct, recv_ct, send_nh, recv_nh,
     send_h2, recv_h2, send_halo, recv_halo, send_rt, recv_rt, send_nw, recv_nw,
 ):
     f32, bf16 = jnp.float32, jnp.bfloat16
@@ -33,6 +33,15 @@
 
     load = pltpu.make_async_copy(tiles_hbm, tiles, tile_sem)
     load.start()
+    local_copies = [
+        pltpu.make_async_copy(src, dst, local_sem.at[i])
+        for i, (src, dst) in enumerate([
+            (fw_hbm, fw_ref), (fh_hbm, fh_ref),
+            (rows_hbm, index_ref.at[0]), (cols_hbm, index_ref.at[1]),
+        ])
+    ]
+    for copy in local_copies:
+        copy.start()
 
     def sig_peer(k):
         return lax.rem(sig + k, n_sig)
@@ -71,14 +80,38 @@
     pending = []
 
     h_copies = [
-        remote(fh_ref, h_blk.at[rows_of(sig, h_rows)], send_h.at[k], recv_h.at[k], {"sig": sig_peer(k)})
+        remote(fh_hbm, h_blk.at[rows_of(sig, h_rows)], send_h.at[k], recv_h.at[k], {"sig": sig_peer(k)})
         for k in range(1, n_sig)
     ]
     w_copies = [
-        remote(fw_ref, w_blk.at[rows_of(build, w_rows)], send_w.at[k], recv_w.at[k], {"build": build_peer(k)})
+        remote(fw_hbm, w_blk.at[rows_of(build, w_rows)], send_w.at[k], recv_w.at[k], {"build": build_peer(k)})
         for k in range(1, n_build)
     ]
     pending += h_copies + w_copies
+    for copy in local_copies:
+        copy.wait()
+    live = count[0, 0]
+    down = lax.broadcasted_iota(jnp.int32, (slots, slots), 0)
+    along = lax.broadcasted_iota(jnp.int32, (slots, slots), 1)
+    for side in range(2):
+        index_row = jnp.broadcast_to(index_ref[side], (slots, slots))
+        index_col = jnp.sum(jnp.where(down == along, index_row, 0), axis=1, keepdims=True)
+        index_col = jnp.broadcast_to(index_col, (slots, slots))
+        same = (index_col == index_row) & (down < along) & (down < live)
+        hit = (index_col == along) & (down < live)
+        lines = [
+            index_row[:1],
+            jnp.max(jnp.where(same, down + 1, 0), axis=0, keepdims=True),
+            jnp.max(jnp.where(hit, down + 1, 0), axis=0, keepdims=True),
+        ]
+        for i, line in enumerate(lines):
+            link_ref[3 * side + i:3 * side + i + 1, 0:slots] = line
+    link_copy = pltpu.make_async_copy(link_ref, meta, local_sem.at[4])
+    link_copy.start()
+
+    def link(line, place, most):
+        return jnp.clip(meta[line, place], 0, most)
+
     h_blk[rows_of(sig, h_rows), :] = fh_ref[...]
     w_blk[rows_of(build, w_rows), :] = fw_ref[...]
     chain_h[0] = jnp.zeros(chain_h.shape[1:], f32)
@@ -100,6 +133,7 @@
     pending += ct_copies
 
     load.wait()
+    link_copy.wait()
     for copy in h_copies:
         copy.wait_recv()
     for c in range(col_tiles):
@@ -113,17 +147,17 @@
         terms = []
         for g in range(GROUP):
             slot = step * GROUP + g
-            row, col = meta[0, slot], meta[1, slot]
+            row, col = link(0, slot, row_tiles - 1), link(3, slot, col_tiles - 1)
             ratio = ratio_of(slot, w_tiles[row], h_tiles[0, col])
             terms.append(jnp.dot(w_turn[row], ratio, preferred_element_type=f32))
         for g in range(GROUP):
             slot = step * GROUP + g
-            chain_h[slot + 1] = chain_h[meta[1, slots + slot]] + terms[g]
+            chain_h[slot + 1] = chain_h[link(4, slot, slots)] + terms[g]
         return carry
 
     lax.fori_loop(0, slots // GROUP, pass_h, 0)
     for c in range(col_tiles):
-        block = chain_h[meta[1, 2 * slots + c]].T
+        block = chain_h[link(5, c, slots)].T
         numer[c * tile:(c + 1) * tile, :] = block
         h_send[c * tile:(c + 1) * tile, :] = block.astype(bf16)
     nh_copies = [
@@ -193,17 +227,17 @@
         terms = []
         for g in range(GROUP):
             slot = step * GROUP + g
-            h = h_tiles[1, meta[1, slot]]
-            ratio = ratio_of(slot, w_tiles[meta[0, slot]], h)
+            h = h_tiles[1, link(3, slot, col_tiles - 1)]
+            ratio = ratio_of(slot, w_tiles[link(0, slot, row_tiles - 1)], h)
             terms.append(jnp.dot(ratio, h, preferred_element_type=f32))
         for g in range(GROUP):
             slot = step * GROUP + g
-            chain_w[slot + 1] = chain_w[meta[0, slots + slot]] + terms[g]
+            chain_w[slot + 1] = chain_w[link(1, slot, slots)] + terms[g]
         return carry
 
     lax.fori_loop(0, slots // GROUP, pass_w, 0)
     for r in range(row_tiles):
-        block = chain_w[meta[0, 2 * slots + r]]
+        block = chain_w[link(2, r, slots)]
         numer[r * tile:(r + 1) * tile, :] = block
         w_send[r * tile:(r + 1) * tile, :] = block.astype(bf16)
     nw_copies = [
@@ -227,28 +261,17 @@
         copy.wait_send()
 
 
-def links(index, tiles, count):
-    slot = jnp.arange(index.shape[0], dtype=jnp.int32)
-    same = (index[:, None] == index[None, :]) & (slot[None, :] < slot[:, None]) & (slot[None, :] < count)
-    before = jnp.max(jnp.where(same, slot[None, :] + 1, 0), axis=1)
-    hit = (jnp.arange(tiles, dtype=jnp.int32)[:, None] == index[None, :]) & (slot[None, :] < count)
-    last = jnp.max(jnp.where(hit, slot[None, :] + 1, 0), axis=1)
-    return jnp.concatenate([index, before, last])
-
-
 def local(n_sig, n_build, tiles, tile_rows, tile_cols, tile_count, factor_w, factor_h, tv_weight):
     tiles = tiles[0, 0]
     slots, tile = tiles.shape[:2]
     w_rows, rank = factor_w.shape
     h_rows = factor_h.shape[0]
     block_rows, block_cols = w_rows * n_build, h_rows * n_sig
-    most = max(block_rows, block_cols) // tile
-    live = tile_count[0, 0]
-    meta = jnp.stack([links(tile_rows[0, 0], most, live), links(tile_cols[0, 0], most, live)])
     vmem, smem = pltpu.VMEM, pltpu.SMEM
     f32, bf16 = jnp.float32, jnp.bfloat16
     dma = pltpu.SemaphoreType.DMA
     in_vmem = pl.BlockSpec(memory_space=pltpu.VMEM)
+    in_hbm = pl.BlockSpec(memory_space=pltpu.HBM)
     in_smem = pl.BlockSpec(memory_space=pltpu.SMEM)
     return pl.pallas_call(
         functools.partial(kernel, n_sig, n_build),
@@ -256,7 +279,7 @@
             jax.ShapeDtypeStruct((w_rows, rank), bf16),
             jax.ShapeDtypeStruct((h_rows, rank), f32),
         ),
-        in_specs=[in_smem, pl.BlockSpec(memory_space=pl.ANY), in_vmem, in_vmem, in_vmem],
+        in_specs=[in_hbm, in_hbm, in_smem, in_hbm, in_hbm, in_hbm, in_vmem],
         out_specs=(in_vmem, in_vmem),
         scratch_shapes=[
             vmem((slots, tile, tile), bf16),
@@ -276,7 +299,12 @@
             vmem((n_sig, 8, rank), f32),
             vmem((n_build, 8, rank), f32),
             vmem((h_rows + 2 * HALO, rank), bf16),
-            dma,
+            vmem((w_rows, rank), bf16),
+            vmem((h_rows, rank), bf16),
+            vmem((2, 1, slots), jnp.int32),
+            vmem((8, 128), jnp.int32),
+            smem((8, 128), jnp.int32),
+            dma, dma((5,)),
             dma((n_build,)), dma((n_build,)),
             dma((n_sig,)), dma((n_sig,)),
             dma((n_sig,)), dma((n_sig,)),
@@ -287,9 +315,9 @@
             dma((n_build,)), dma((n_build,)),
         ],
         compiler_params=pltpu.CompilerParams(
-            collective_id=0, has_side_effects=True, vmem_limit_bytes=40 * 1024 * 1024
+            collective_id=0, has_side_effects=True, vmem_limit_bytes=60 * 1024 * 1024
         ),
-    )(meta, tiles, factor_w, factor_h, tv_weight[None, :])
+    )(tile_rows[0], tile_cols[0], tile_count, tiles, factor_w, factor_h, tv_weight[None, :])
 
 
 def solution(mesh):

time: 73.5 us -> 66.9 us (0.910)
  local copies, waits for them, and re-layouts: 6 us -> 3.24 us
  other arithmetic: 2.52 us -> 0 us
  Pallas kernels: 63.5 us -> 62.2 us
    unnamed x10 -> x2, local copies, waits for them, and re-layouts: 6 us -> 3.24 us
    reduce_max x2 -> x0, other arithmetic: 1.75 us -> none  [the longest x1 0.93 us: links(): before = jnp.max(jnp.where(same, slot[None, :] + 1, 0), axis=1)]
    pallas_call x1, Pallas kernels: 63.5 us -> 62.2 us  [local(): pl.pallas_call(functools.partial(kernel, n_sig, n_build), out_shape=(jax....]
    another operation x2 -> x0, other arithmetic: 0.76 us -> none  [local(): jnp.stack([links(tile_rows[0, 0], most, live), links(tile_cols[0, 0], mos...]
where the time goes in v2:
time: 66.9 us; the launch traced here: 66.7 us
  Pallas kernels  62.2 us (93%)
  local copies, waits for them, and re-layouts  3.24 us (5%)
  between operations  1.29 us (2%)
    pallas_call x1, Pallas kernels, local(): pl.pallas_call(functools.partial(kernel, n_sig, n_build), out_shape=(jax....  62.2 us
    unnamed x2, local copies, waits for them, and re-layouts  3.24 us

profile of v2, /device:TPU:21, one launch (start us, length us, event | category | flops | bytes accessed | tf_op | source)
XLA Modules:
  0.0 66.7 jit_solution(13254842272256248809)
XLA Ops:
  1.3 62.2 %shard_map.86 = (bf16[512,128]{1,0:T(8,128)(2,1)}, f32[512,128]{1,0:T(8,128)}) custom-call(s32[1,32]{1,0:T(1,128)} %bitcast.5, s32[1,32]{1,0:T(1,128)} %bitcast.6, s32[1,1]{1,0:T(1,128)S(6)} %copy.11.count, bf16[32,256,256]{2,1,0:T(8,128)(2,1)} %bitcast.4, bf16[512,128]{1,0:T(8,128)(2,1)} %fw_hbm.1, bf16[512,128]{1,0:T(8,128)(2,1)} %fh_hbm.1, f32[1,128]{1,0:T(1,128)} %bitcast.7), custom_call_target="tpu_custom_call" | custom-call | tf_op jit(solution)/shard_map/pallas_call | solution.py:276
  63.5 1.6 %copy.12 = bf16[512,128]{1,0:T(8,128)(2,1)} copy(bf16[512,128]{1,0:T(8,128)(2,1)} %get-tuple-element.4) | data formatting | bytes 262144
  65.0 1.7 %copy.13 = f32[512,128]{1,0:T(8,128)} copy(f32[512,128]{1,0:T(8,128)} %get-tuple-element.5) | data formatting | bytes 524288

commit v3 on v2

--- a/solution.py
+++ b/solution.py
@@ -20,7 +20,7 @@
     w_out, smooth_out,
     tiles, w_blk, w_turn, h_blk, h_next, w_tiles, h_tiles, chain_h, chain_w, numer,
     h_send, h_recv, w_send, w_recv, col_part, row_part, ext,
-    fw_ref, fh_ref, index_ref, link_ref, meta, tile_sem, local_sem, send_w, recv_w, send_h, recv_h, send_ct, recv_ct, send_nh, recv_nh,
+    fw_ref, fh_ref, index_ref, link_ref, meta, h_hop, send_on, recv_hop, tile_sem, local_sem, send_w, recv_w, send_h, recv_h, send_ct, recv_ct, send_nh, recv_nh,
     send_h2, recv_h2, send_halo, recv_halo, send_rt, recv_rt, send_nw, recv_nw,
 ):
     f32, bf16 = jnp.float32, jnp.bfloat16
@@ -66,11 +66,14 @@
     pl.semaphore_signal(barrier, inc=1, device_id=at(below), device_id_type=MESH)
     pl.semaphore_wait(barrier, n_sig + n_build)
 
-    def remote(src, dst, send, recv, device):
-        copy = pltpu.make_async_remote_copy(
+    def describe(src, dst, send, recv, device):
+        return pltpu.make_async_remote_copy(
             src_ref=src, dst_ref=dst, send_sem=send, recv_sem=recv,
             device_id=device, device_id_type=MESH,
         )
+
+    def remote(src, dst, send, recv, device):
+        copy = describe(src, dst, send, recv, device)
         copy.start()
         return copy
 
@@ -78,16 +81,57 @@
         return pl.ds(pl.multiple_of(place * rows, rows), rows)
 
     pending = []
-
-    h_copies = [
-        remote(fh_hbm, h_blk.at[rows_of(sig, h_rows)], send_h.at[k], recv_h.at[k], {"sig": sig_peer(k)})
-        for k in range(1, n_sig)
-    ]
+    relay = n_sig == 4
+    order = [2, 1, 3] if relay else list(range(1, n_sig))
+    is_end = (sig == 0) | (sig == n_sig - 1)
+    far = n_sig - 1 - sig
+    inner = jnp.where(sig * 2 < n_sig, 1, n_sig - 2)
+    outer = jnp.where(sig * 2 < n_sig, 0, n_sig - 1)
+
+    def when(condition, action):
+        if condition is None:
+            action()
+        else:
+            pl.when(condition)(action)
+
+    def sends(k):
+        if not relay or k == 2:
+            return None
+        return sig != (0 if k == n_sig - 1 else n_sig - 1)
+
+    class Gather:
+        def __init__(self, src, block, send, recv, send_on):
+            mine = block.at[rows_of(sig, h_rows)]
+            self.copies = {
+                k: describe(src, mine, send.at[k], recv.at[k], {"sig": sig_peer(k)}) for k in order
+            }
+            for k in order:
+                when(sends(k), self.copies[k].start)
+            crossed = block.at[rows_of(sig_peer(2), h_rows)]
+            self.on = [
+                describe(crossed, crossed, send_on, recv.at[k], {"sig": outer}) for k in (1, n_sig - 1)
+            ] if relay else []
+
+        def receive(self):
+            for k in order:
+                self.copies[k].wait_recv()
+                if relay and k == 2:
+                    when(sig == 1, self.on[0].start)
+                    when(sig == n_sig - 2, self.on[1].start)
+
+        def finish(self):
+            for k in order:
+                when(sends(k), self.copies[k].wait_send)
+            if relay:
+                when(sig == 1, self.on[0].wait_send)
+                when(sig == n_sig - 2, self.on[1].wait_send)
+
+    gather_h = Gather(fh_hbm, h_blk, send_h, recv_h, send_on.at[0])
     w_copies = [
         remote(fw_hbm, w_blk.at[rows_of(build, w_rows)], send_w.at[k], recv_w.at[k], {"build": build_peer(k)})
         for k in range(1, n_build)
     ]
-    pending += h_copies + w_copies
+    pending += w_copies
     for copy in local_copies:
         copy.wait()
     live = count[0, 0]
@@ -134,8 +178,7 @@
 
     load.wait()
     link_copy.wait()
-    for copy in h_copies:
-        copy.wait_recv()
+    gather_h.receive()
     for c in range(col_tiles):
         h_tiles[0, c] = h_blk[c * tile:(c + 1) * tile, :]
 
@@ -160,24 +203,40 @@
         block = chain_h[link(5, c, slots)].T
         numer[c * tile:(c + 1) * tile, :] = block
         h_send[c * tile:(c + 1) * tile, :] = block.astype(bf16)
-    nh_copies = [
-        remote(h_send.at[rows_of(sig_peer(k), h_rows)], h_recv.at[sig], send_nh.at[k], recv_nh.at[k],
-               {"sig": sig_peer(k)})
-        for k in range(1, n_sig)
-    ]
-    pending += nh_copies
+    nh_copies = {
+        k: describe(h_send.at[rows_of(sig_peer(k), h_rows)], h_recv.at[sig], send_nh.at[k], recv_nh.at[k],
+                    {"sig": sig_peer(k)})
+        for k in order
+    }
+    hop = describe(h_send.at[rows_of(far, h_rows)], h_hop, send_on.at[2], recv_hop, {"sig": inner})
+    if relay:
+        when(is_end, hop.start)
+    for k in order:
+        when(is_end if relay and k == 2 else sends(k), nh_copies[k].start)
+    if relay:
+        @pl.when(jnp.logical_not(is_end))
+        def _():
+            hop.wait_recv()
+            crossing = rows_of(sig_peer(2), h_rows)
+            h_send[crossing, :] = (numer[crossing, :] + h_hop[...].astype(f32)).astype(bf16)
+            nh_copies[2].start()
     for copy in ct_copies:
         copy.wait_recv()
     col_sum = col_part[0]
     for k in range(1, n_sig):
         col_sum += col_part[k]
     col_total = jnp.sum(col_sum, axis=0, keepdims=True)
-    share = numer[rows_of(sig, h_rows), :]
-    for k in range(1, n_sig):
-        nh_copies[k - 1].wait_recv()
-        share += h_recv[sig_peer(n_sig - k)].astype(f32)
+    mine = rows_of(sig, h_rows)
+
+    def add(k):
+        nh_copies[k].wait_recv()
+        numer[mine, :] += h_recv[sig_peer(n_sig - k)].astype(f32)
+
+    for k in order[::-1]:
+        arrives = None if not relay or k == 2 else sig != (n_sig - 1 if k == n_sig - 1 else 0)
+        when(arrives, functools.partial(add, k))
+    share = numer[mine, :]
     h_new = (fh_ref[...].astype(f32) * share / col_total).astype(bf16)
-    mine = rows_of(sig, h_rows)
     h_next[mine, :] = h_new
     ext[HALO:HALO + h_rows, :] = h_new
     halo_copies = [
@@ -185,11 +244,8 @@
         remote(ext.at[HALO:2 * HALO], ext.at[HALO + h_rows:2 * HALO + h_rows],
                send_halo.at[1], recv_halo.at[1], at(below)),
     ]
-    h2_copies = [
-        remote(h_next.at[mine], h_next.at[mine], send_h2.at[k], recv_h2.at[k], {"sig": sig_peer(k)})
-        for k in range(1, n_sig)
-    ]
-    pending += halo_copies + h2_copies
+    gather_next = Gather(h_next.at[mine], h_next, send_h2, recv_h2, send_on.at[1])
+    pending += halo_copies
 
     for copy in halo_copies:
         copy.wait_recv()
@@ -209,8 +265,7 @@
     smooth = signal - pltpu.roll(dual, 1, 0) + dual
     smooth_out[...] = smooth[HALO:HALO + h_rows, :]
 
-    for copy in h2_copies:
-        copy.wait_recv()
+    gather_next.receive()
     part = jnp.zeros((8, w_blk.shape[1]), f32)
     for c in range(col_tiles):
         block = h_next[c * tile:(c + 1) * tile, :]
@@ -259,6 +314,12 @@
     w_out[...] = (fw_ref[...].astype(f32) * share / row_total).astype(bf16)
     for copy in pending:
         copy.wait_send()
+    gather_h.finish()
+    gather_next.finish()
+    for k in order:
+        when(sends(k), nh_copies[k].wait_send)
+    if relay:
+        when(is_end, hop.wait_send)
 
 
 def local(n_sig, n_build, tiles, tile_rows, tile_cols, tile_count, factor_w, factor_h, tv_weight):
@@ -304,6 +365,8 @@
             vmem((2, 1, slots), jnp.int32),
             vmem((8, 128), jnp.int32),
             smem((8, 128), jnp.int32),
+            vmem((h_rows, rank), bf16),
+            dma((3,)), dma,
             dma, dma((5,)),
             dma((n_build,)), dma((n_build,)),
             dma((n_sig,)), dma((n_sig,)),

time: 66.9 us -> 63.5 us (0.949)
  the two profiles are of different devices: /device:TPU:21 before, /device:TPU:1 now
where the time goes in v3:
time: 63.5 us; the launch traced here: 63.3 us
  Pallas kernels  58.8 us (93%)
  local copies, waits for them, and re-layouts  3.24 us (5%)
  between operations  1.29 us (2%)
    pallas_call x1, Pallas kernels, local(): pl.pallas_call(functools.partial(kernel, n_sig, n_build), out_shape=(jax....  58.8 us
    unnamed x2, local copies, waits for them, and re-layouts  3.24 us

profile of v3, /device:TPU:1, one launch (start us, length us, event | category | flops | bytes accessed | tf_op | source)
XLA Modules:
  0.0 63.3 jit_solution(6134390740103271214)
XLA Ops:
  1.3 58.8 %shard_map.86 = (bf16[512,128]{1,0:T(8,128)(2,1)}, f32[512,128]{1,0:T(8,128)}) custom-call(s32[1,32]{1,0:T(1,128)} %bitcast.5, s32[1,32]{1,0:T(1,128)} %bitcast.6, s32[1,1]{1,0:T(1,128)S(6)} %copy.11.count, bf16[32,256,256]{2,1,0:T(8,128)(2,1)} %bitcast.4, bf16[512,128]{1,0:T(8,128)(2,1)} %fw_hbm.1, bf16[512,128]{1,0:T(8,128)(2,1)} %fh_hbm.1, f32[1,128]{1,0:T(1,128)} %bitcast.7), custom_call_target="tpu_custom_call" | custom-call | tf_op jit(solution)/shard_map/pallas_call | solution.py:337
  60.0 1.6 %copy.12 = bf16[512,128]{1,0:T(8,128)(2,1)} copy(bf16[512,128]{1,0:T(8,128)(2,1)} %get-tuple-element.4) | data formatting | bytes 262144
  61.6 1.7 %copy.13 = f32[512,128]{1,0:T(8,128)} copy(f32[512,128]{1,0:T(8,128)} %get-tuple-element.5) | data formatting | bytes 524288

commit v4 on v3

--- a/solution.py
+++ b/solution.py
@@ -10,7 +10,7 @@
 TV_STEPS = 16
 TAU = 0.25
 HALO = 32
-GROUP = 8
+GROUP = 16
 MESH = pl.DeviceIdType.MESH
 
 

time: 63.5 us -> 62.4 us (0.983)
  Pallas kernels: 58.8 us -> 57.6 us
    pallas_call x1, Pallas kernels: 58.8 us -> 57.6 us  [local(): pl.pallas_call(functools.partial(kernel, n_sig, n_build), out_shape=(jax....]
where the time goes in v4:
time: 62.4 us; the launch traced here: 62.2 us
  Pallas kernels  57.6 us (92%)
  local copies, waits for them, and re-layouts  3.24 us (5%)
  between operations  1.29 us (2%)
    pallas_call x1, Pallas kernels, local(): pl.pallas_call(functools.partial(kernel, n_sig, n_build), out_shape=(jax....  57.6 us
    unnamed x2, local copies, waits for them, and re-layouts  3.24 us

profile of v4, /device:TPU:1, one launch (start us, length us, event | category | flops | bytes accessed | tf_op | source)
XLA Modules:
  0.0 62.2 jit_solution(12463982899758229911)
XLA Ops:
  1.3 57.6 %shard_map.86 = (bf16[512,128]{1,0:T(8,128)(2,1)}, f32[512,128]{1,0:T(8,128)}) custom-call(s32[1,32]{1,0:T(1,128)} %bitcast.5, s32[1,32]{1,0:T(1,128)} %bitcast.6, s32[1,1]{1,0:T(1,128)S(6)} %copy.11.count, bf16[32,256,256]{2,1,0:T(8,128)(2,1)} %bitcast.4, bf16[512,128]{1,0:T(8,128)(2,1)} %fw_hbm.1, bf16[512,128]{1,0:T(8,128)(2,1)} %fh_hbm.1, f32[1,128]{1,0:T(1,128)} %bitcast.7), custom_call_target="tpu_custom_call" | custom-call | tf_op jit(solution)/shard_map/pallas_call | solution.py:337
  58.9 1.6 %copy.12 = bf16[512,128]{1,0:T(8,128)(2,1)} copy(bf16[512,128]{1,0:T(8,128)(2,1)} %get-tuple-element.4) | data formatting | bytes 262144
  60.5 1.7 %copy.13 = f32[512,128]{1,0:T(8,128)} copy(f32[512,128]{1,0:T(8,128)} %get-tuple-element.5) | data formatting | bytes 524288

commit v5 on v4

--- a/solution.py
+++ b/solution.py
@@ -291,15 +291,21 @@
         return carry
 
     lax.fori_loop(0, slots // GROUP, pass_w, 0)
-    for r in range(row_tiles):
-        block = chain_w[link(2, r, slots)]
-        numer[r * tile:(r + 1) * tile, :] = block
-        w_send[r * tile:(r + 1) * tile, :] = block.astype(bf16)
-    nw_copies = [
-        remote(w_send.at[rows_of(build_peer(k), w_rows)], w_recv.at[build], send_nw.at[k], recv_nw.at[k],
-               {"build": build_peer(k)})
-        for k in range(1, n_build)
-    ]
+    per_shard = w_rows // tile
+    nw_copies = []
+    for k in list(range(1, n_build)) + [0]:
+        owner = build_peer(k)
+        for i in range(per_shard):
+            block = chain_w[link(2, owner * per_shard + i, slots)]
+            if k:
+                w_send[rows_of(owner * per_shard + i, tile), :] = block.astype(bf16)
+            else:
+                numer[rows_of(owner * per_shard + i, tile), :] = block
+        if k:
+            nw_copies.append(
+                remote(w_send.at[rows_of(owner, w_rows)], w_recv.at[build], send_nw.at[k], recv_nw.at[k],
+                       {"build": owner})
+            )
     pending += nw_copies
     for copy in rt_copies:
         copy.wait_recv()

time: 62.4 us -> 62.3 us (level)
  no operation moved by 1% of the time
where the time goes in v5:
time: 62.3 us; the launch traced here: 62.1 us
  Pallas kernels  57.6 us (92%)
  local copies, waits for them, and re-layouts  3.24 us (5%)
  between operations  1.29 us (2%)
    pallas_call x1, Pallas kernels, local(): pl.pallas_call(functools.partial(kernel, n_sig, n_build), out_shape=(jax....  57.6 us
    unnamed x2, local copies, waits for them, and re-layouts  3.24 us

profile of v5, /device:TPU:1, one launch (start us, length us, event | category | flops | bytes accessed | tf_op | source)
XLA Modules:
  0.0 62.1 jit_solution(10061402078229444379)
XLA Ops:
  1.3 57.6 %shard_map.86 = (bf16[512,128]{1,0:T(8,128)(2,1)}, f32[512,128]{1,0:T(8,128)}) custom-call(s32[1,32]{1,0:T(1,128)} %bitcast.5, s32[1,32]{1,0:T(1,128)} %bitcast.6, s32[1,1]{1,0:T(1,128)S(6)} %copy.11.count, bf16[32,256,256]{2,1,0:T(8,128)(2,1)} %bitcast.4, bf16[512,128]{1,0:T(8,128)(2,1)} %fw_hbm.1, bf16[512,128]{1,0:T(8,128)(2,1)} %fh_hbm.1, f32[1,128]{1,0:T(1,128)} %bitcast.7), custom_call_target="tpu_custom_call" | custom-call | tf_op jit(solution)/shard_map/pallas_call | solution.py:343
  58.9 1.6 %copy.12 = bf16[512,128]{1,0:T(8,128)(2,1)} copy(bf16[512,128]{1,0:T(8,128)(2,1)} %get-tuple-element.4) | data formatting | bytes 262144
  60.4 1.7 %copy.13 = f32[512,128]{1,0:T(8,128)} copy(f32[512,128]{1,0:T(8,128)} %get-tuple-element.5) | data formatting | bytes 524288
